TPU v7x, 32 devices: a whole 2x2x4 slice. The times are simulated.
32 devices in a mesh: parts: 2 (over y), section: 4 (over z), seq: 2 (over core), tensor: 2 (over x).
Axes of the slice: x: 2, y: 2, z: 4, core: 2. Of those that a mesh axis runs over, the one named last changes fastest.
Arguments:
- hidden_state: bfloat16 [8, 1024, 5120], P(('parts', 'section'), 'seq', 'tensor'), parts along dimension 0, may hold values from -6 to 6
- frame_query: bfloat16 [8, 1024, 2560], P(('parts', 'section'), 'seq', 'tensor'), parts along dimension 0, may hold values from -12 to 12
- frame_key: bfloat16 [8, 1024, 2560], P(('parts', 'section'), 'seq', 'tensor'), parts along dimension 0, may hold values from -6 to 6
- frame_value: bfloat16 [8, 1024, 2560], P(('parts', 'section'), 'seq', 'tensor'), parts along dimension 0, may hold values from -6 to 6
- cache_key: bfloat16 [2048, 2560], P(('parts', 'section', 'seq'), 'tensor'), parts along dimension 0, may hold values from -6 to 6
- cache_value: bfloat16 [2048, 2560], P(('parts', 'section', 'seq'), 'tensor'), parts along dimension 0, may hold values from -6 to 6
- out_weight: bfloat16 [2560, 5120], P('tensor'), may hold values from -0.8984375 to 0.8984375
- level_gate: float32 [8, 5120], P(None, 'tensor'), may hold values from 0.5 to 1.5
- noise_level: int32 [8], P('parts'), parts along dimension 0, may hold values from 0 to 7
- frame_position: int32 [8], P('parts'), parts along dimension 0, may hold values from 0 to 3, each once
- cached_count: int32 [2], P('parts'), parts along dimension 0, may hold values from 256 to 1024
Outputs:
- advanced: bfloat16 [8, 1024, 5120], P(('parts', 'section'), 'seq', 'tensor'), parts along dimension 0
There are 2 independent parts, one for each index of `parts`. A program takes and returns all parts, laid end to end along the dimension named above; an argument that names none is the same for every part. Nothing has to cross between parts.
Inputs may be any that keep to these rules, and one draw needn't show every extreme that they name: `frame_position`: a permutation: every section holds a different frame position.
All inputs are finite; a program needn't handle non-finite values.
Results may differ from a plain program's by a relative error of at most 0.015.
Values may be sent and summed in bfloat16 or wider, within the bound.
A program may use at most 128 MiB of HBM per device.

v0:
```python
import jax
import jax.numpy as jnp
from jax import lax
from jax.sharding import PartitionSpec as P

HD = 128


masked_score = -1e30


def shifted(block, axis, distance):
    devices = range(lax.axis_size(axis))
    route = [((i - distance) % len(devices), i) for i in devices]
    return lax.ppermute(block, axis, route)


def attend(running, queries, key_rows, value_rows, visible):
    highest, total, accumulated = running
    head_count = queries.shape[1]
    key_heads = key_rows.reshape(key_rows.shape[0], head_count, HD)
    value_heads = value_rows.reshape(value_rows.shape[0], head_count, HD)
    scores = jnp.einsum(
        "thd,nhd->thn", queries, key_heads, preferred_element_type=jnp.float32
    ) * HD ** (-0.5)
    if visible is not None:
        scores = jnp.where(visible[None, None, :], scores, masked_score)
    raised = jnp.maximum(highest, jnp.max(scores, axis=2))
    factor = jnp.exp(highest - raised)
    exponent = jnp.exp(scores - raised[:, :, None])
    total = total * factor + jnp.sum(exponent, axis=2)
    weights = exponent.astype(jnp.bfloat16)
    accumulated = accumulated * factor[:, :, None] + jnp.einsum(
        "thn,nhd->thd", weights, value_heads, preferred_element_type=jnp.float32
    )
    return (raised, total, accumulated)


def on_device(
    hidden_state,
    frame_query,
    frame_key,
    frame_value,
    cache_key,
    cache_value,
    out_weight,
    level_gate,
    noise_level,
    frame_position,
    cached_count,
):
    section_count = lax.axis_size("section")
    section_index = lax.axis_index("section")
    hidden_state, frame_query, frame_key, frame_value = shifted(
        (hidden_state, frame_query, frame_key, frame_value), "section", 1
    )
    source_section = (section_index + section_count - 1) % section_count
    one_hot = (jnp.arange(section_count, dtype=jnp.int32) == source_section).astype(jnp.int32)
    level_now = jnp.sum(one_hot * noise_level)
    position = jnp.sum(one_hot * frame_position)
    row_limit = cached_count[0]
    level_pick = jnp.arange(level_gate.shape[0], dtype=jnp.int32) == level_now
    gate_row = jnp.sum(jnp.where(level_pick[:, None], level_gate, 0.0), axis=0)
    tok_rows = frame_query.shape[1]
    head_count = frame_query.shape[2] // HD
    queries = frame_query[0].reshape(tok_rows, head_count, HD)
    frame_keys, frame_values = (
        lax.all_gather(frame_key[0], "seq", axis=0, tiled=True),
        lax.all_gather(frame_value[0], "seq", axis=0, tiled=True),
    )
    start_state = (
        jnp.full((tok_rows, head_count), masked_score, jnp.float32),
        jnp.zeros((tok_rows, head_count), jnp.float32),
        jnp.zeros((tok_rows, head_count, HD), jnp.float32),
    )
    running = attend(start_state, queries, frame_keys, frame_values, None)
    cache_rows = cache_key.shape[0] * lax.axis_size("seq")
    key_rows = lax.all_gather(cache_key, ("section", "seq"), axis=0, tiled=True)
    value_rows = lax.all_gather(cache_value, ("section", "seq"), axis=0, tiled=True)
    row_count = key_rows.shape[0]
    row_index = jnp.arange(row_count, dtype=jnp.int32)
    slot_index = row_index // cache_rows
    visible = (slot_index < position) & (row_index < row_limit)
    block_rows = 512
    block_count = row_count // block_rows

    def block_step(inner_state, block_parts):
        return (attend(inner_state, queries, block_parts[0], block_parts[1], block_parts[2]), None)

    result, unused = lax.scan(
        block_step,
        running,
        (
            key_rows.reshape(block_count, block_rows, -1),
            value_rows.reshape(block_count, block_rows, -1),
            visible.reshape(block_count, block_rows),
        ),
    )
    running = result
    highest, total, accumulated = running
    attended = (
        (accumulated / total[:, :, None]).astype(jnp.bfloat16).reshape(tok_rows, head_count * HD)
    )
    partial_value = jnp.dot(attended, out_weight, preferred_element_type=jnp.float32)
    branch_sum = lax.psum_scatter(
        partial_value.astype(jnp.bfloat16), "tensor", scatter_dimension=1, tiled=True
    ).astype(jnp.float32)
    updated = (hidden_state[0].astype(jnp.float32) + gate_row[None, :] * branch_sum).astype(
        jnp.bfloat16
    )[None]
    return updated


def solution(mesh):
    placed = (
        P(("parts", "section"), "seq", "tensor"),
        P(("parts", "section"), "seq", "tensor"),
        P(("parts", "section"), "seq", "tensor"),
        P(("parts", "section"), "seq", "tensor"),
        P(("parts", "section", "seq"), "tensor"),
        P(("parts", "section", "seq"), "tensor"),
        P("tensor", None),
        P(None, "tensor"),
        P("parts"),
        P("parts"),
        P("parts"),
    )
    return jax.shard_map(
        on_device,
        mesh=mesh,
        in_specs=placed,
        out_specs=P(("parts", "section"), "seq", "tensor"),
        check_vma=False,
    )
```

profile of v0, /device:TPU:1, one launch (start us, length us, event | category | flops | bytes accessed | tf_op | source)
XLA Modules:
  0.0 300.4 jit_solution(9489797371300131060)
XLA Ops:
  6.5 0.0 copy-start.2
  6.5 0.0 all-gather.11.cloned.1.call-start
  6.5 1.7 copy.29
  8.3 2.2 collective-permute-start.1
  10.4 30.6 %collective-permute-done.1 = bf16[1,512,1280]{1,2,0:T(8,128)(2,1)} collective-permute-done((bf16[1,512,1280]{1,2,0:T(8,128)(2,1)S(1)}, bf16[1,512,1280]{1,2,0:T(8,128)(2,1)}, u32[]{:S(2)}, u32[]{:S(2)}) %collective-permute-start.1) | collective-permute-done | bytes 1310752 | tf_op jit(solution)/shard_map/ppermute | solution.py:15
  41.1 0.0 copy-start.3
  41.1 0.0 all-gather.11.cloned.1.call-update
  41.1 0.0 all-gather.13.cloned.1.call-start
  41.1 0.0 copy-done.2
  41.2 1.5 copy.33
  42.6 0.0 collective-permute-start.3
  42.6 31.0 %collective-permute-done.3 = bf16[1,512,1280]{1,2,0:T(8,128)(2,1)S(1)} collective-permute-done((bf16[1,512,1280]{1,2,0:T(8,128)(2,1)}, bf16[1,512,1280]{1,2,0:T(8,128)(2,1)S(1)}, u32[]{:S(2)}, u32[]{:S(2)}) %collective-permute-start.3) | collective-permute-done | bytes 1310752 | tf_op jit(solution)/shard_map/ppermute | solution.py:15
  73.7 1.1 copy-done.4
  74.7 0.0 all-gather.13.cloned.1.call-update
  74.8 0.0 all-gather.7.cloned.1.call-start
  74.8 0.7 all-gather.7.cloned.1.call-update
  75.5 0.0 all-gather.9.cloned.1.call-start
  75.6 0.0 copy-done.3
  75.6 1.5 copy.30
  77.0 0.0 collective-permute-start.2
  77.0 0.0 all-gather.9.cloned.1.call-update
  77.1 0.0 reduce-scatter.2.cloned.1.call-start
  77.8 0.0 copy-done.6
  77.8 0.6 fusion.25
  78.4 0.6 compare_and_fusion
  79.0 34.4 %collective-permute-done.2 = bf16[1,512,1280]{1,2,0:T(8,128)(2,1)S(1)} collective-permute-done((bf16[1,512,1280]{1,2,0:T(8,128)(2,1)}, bf16[1,512,1280]{1,2,0:T(8,128)(2,1)S(1)}, u32[]{:S(2)}, u32[]{:S(2)}) %collective-permute-start.2) | collective-permute-done | bytes 1310752 | tf_op jit(solution)/shard_map/ppermute | solution.py:15
  113.3 1.5 copy.38
  114.9 4.7 %bitcast_reduce_fusion.1 = (f32[512,10]{0,1:T(8,128)S(1)}, f32[10,1024,512]{2,1,0:T(8,128)S(1)}) fusion(bf16[1024,10,128]{0,2,1:T(8,128)(2,1)} %bitcast.75, bf16[512,10,128]{0,2,1:T(8,128)(2,1)S(1)} %bitcast.74), kind=kOutput, calls=%fused_computation.20 | convolution fusion | flops 1352657920 | bytes 24924160 | tf_op jit(solution)/shard_map/thd,nhd->thn/dot_general | solution.py:23
  119.6 0.0 copy-start.1
  119.6 3.5 %fusion.15 = f32[512,10]{0,1:T(8,128)S(1)} fusion(f32[10,1024,512]{2,1,0:T(8,128)S(1)} %get-tuple-element.99, f32[512,10]{0,1:T(8,128)S(1)} %broadcast_maximum_fusion), kind=kLoop, calls=%fused_computation.23 | loop fusion | flops 15723520 | bytes 21012480 | tf_op jit(solution)/shard_map/reduce_sum | solution.py:31
  123.1 3.5 %copy-done.1 = f32[10,1024,512]{2,1,0:T(8,128)} copy-done((f32[10,1024,512]{2,1,0:T(8,128)}, f32[10,1024,512]{2,1,0:T(8,128)S(1)}, u32[]{:S(2)}) %copy-start.1) | copy-done | bytes 20971544
  126.7 0.0 all-gather.13.cloned.1.call-done
  126.7 10.4 %bitcast_add_fusion.1 = f32[512,10,128]{2,0,1:T(8,128)S(1)} fusion(bf16[1024,10,128]{0,2,1:T(8,128)(2,1)} %bitcast.76, f32[10,1024,512]{2,1,0:T(8,128)} %copy-done.1, f32[512,10]{0,1:T(8,128)S(1)} %broadcast_maximum_fusion, f32[512,10]{0,1:T(8,128)S(1)} %get-tuple-element.96), kind=kOutput, calls=%fused_computation.31 | convolution fusion | flops 1358561280 | bytes 26255360 | tf_op jit(solution)/shard_map/thn,nhd->thd/dot_general | solution.py:33
  137.1 2.1 copy.36
  139.2 26.6 %all-gather.9.cloned.1.call-done = bf16[1024,1280]{1,0:T(8,128)(2,1)} async-done(((bf16[128,1280]{1,0:T(8,128)(2,1)}), bf16[1024,1280]{1,0:T(8,128)(2,1)}) %all-gather.9.cloned.1.call-update) | async-done | bytes 2621456 | tf_op jit(solution)/shard_map/all_gather | solution.py:79
  165.8 44.0 %while.14 = (s32[]{:T(128)}, f32[512,10]{0,1:T(8,128)S(1)}, f32[512,10]{0,1:T(8,128)S(1)}, f32[512,10,128]{0,2,1:T(8,128)}, pred[2,512]{1,0:T(4,128)(4,1)S(1)}, ...) while((s32[]{:T(128)}, f32[512,10]{0,1:T(8,128)S(1)}, ...), condition=%wide.region_8.9_spmd, body=%wide.region_5.8_spmd.sunk | while | flops 1372334080 | bytes 93391496 | solution.py:90
  165.8 2.9 constant_dynamic-slice_fusion.3
  168.8 1.6 copy.50
  170.4 3.8 %bitcast_reduce_fusion.3 = (f32[512,10]{0,1:T(8,128)S(1)}, f32[10,512,512]{2,1,0:T(8,128)S(1)}) fusion(pred[512]{0:T(512)(128)(4,1)S(1)} %dynamic-slice_reduce_fusion.2, bf16[512,10,128]{0,2,1:T(8,128)(2,1)S(1)} %bitcast.70, bf16[512,10,128]{2,0,1:T(8,128)(2,1)} %get-tuple-element.185), kind=kOutput, calls=%fused_computation.1.clone.1 | convolution fusion | flops 678947840 | bytes 13128192 | tf_op jit(solution)/shard_map/while/body/eval_jaxpr/thd,nhd->thn/dot_general | solution.py:23
  174.2 0.0 copy-start
  174.2 2.2 fusion.45
  176.4 1.7 copy-done
  178.2 0.7 copy.51
  178.8 9.0 %bitcast_add_fusion.3 = f32[512,10,128]{0,2,1:T(8,128)} fusion(f32[512,10,128]{0,2,1:T(8,128)} %get-tuple-element.173, bf16[512,10,128]{0,2,1:T(8,128)(2,1)S(1)} %bitcast.69, f32[10,512,512]{2,1,0:T(8,128)} %copy-done, f32[512,10]{0,1:T(8,128)S(1)} %max.4, pred[512]{0:T(512)(128)(4,1)S(1)} %dynamic-slice_reduce_fusion.2, ...), kind=kOutput, calls=%fused_computation.11.clone.1 | convolution fusion | flops 682885120 | bytes 17080832 | tf_op jit(solution)/shard_map/while/body/eval_jaxpr/thn,nhd->thd/dot_general | solution.py:33
  187.8 2.9 constant_dynamic-slice_fusion.3
  190.8 1.6 copy.50
  192.4 3.8 %bitcast_reduce_fusion.3 = (f32[512,10]{0,1:T(8,128)S(1)}, f32[10,512,512]{2,1,0:T(8,128)S(1)}) fusion(pred[512]{0:T(512)(128)(4,1)S(1)} %dynamic-slice_reduce_fusion.2, bf16[512,10,128]{0,2,1:T(8,128)(2,1)S(1)} %bitcast.70, bf16[512,10,128]{2,0,1:T(8,128)(2,1)} %get-tuple-element.185), kind=kOutput, calls=%fused_computation.1.clone.1 | convolution fusion | flops 678947840 | bytes 13128192 | tf_op jit(solution)/shard_map/while/body/eval_jaxpr/thd,nhd->thn/dot_general | solution.py:23
  196.2 0.0 copy-start
  196.2 2.2 fusion.45
  198.4 1.7 copy-done
  200.2 0.7 copy.51
  200.8 9.0 %bitcast_add_fusion.3 = f32[512,10,128]{0,2,1:T(8,128)} fusion(f32[512,10,128]{0,2,1:T(8,128)} %get-tuple-element.173, bf16[512,10,128]{0,2,1:T(8,128)(2,1)S(1)} %bitcast.69, f32[10,512,512]{2,1,0:T(8,128)} %copy-done, f32[512,10]{0,1:T(8,128)S(1)} %max.4, pred[512]{0:T(512)(128)(4,1)S(1)} %dynamic-slice_reduce_fusion.2, ...), kind=kOutput, calls=%fused_computation.11.clone.1 | convolution fusion | flops 682885120 | bytes 17080832 | tf_op jit(solution)/shard_map/while/body/eval_jaxpr/thn,nhd->thd/dot_general | solution.py:33
  209.8 2.1 divide_convert_fusion
  211.9 13.5 %convolution_convert_fusion = bf16[512,5120]{1,0:T(8,128)(2,1)} fusion(bf16[512,1280]{0,1:T(8,128)(2,1)S(1)} %bitcast.77, bf16[1280,5120]{1,0:T(8,128)(2,1)} %param.19), kind=kOutput, calls=%fused_computation.27 | convolution fusion | flops 6713507840 | bytes 19660800 | tf_op jit(solution)/shard_map/dot_general | solution.py:104
  225.4 0.0 reduce-scatter.2.cloned.1.call-update
  225.5 0.6 collective-permute-start
  226.1 0.0 copy-done.7
  226.1 0.6 fusion.24
  226.7 0.6 iota_compare_fusion
  227.4 0.0 copy-done.5
  227.4 0.1 select_reduce_fusion
  227.5 58.2 %collective-permute-done = bf16[1,512,2560]{2,1,0:T(8,128)(2,1)S(1)} collective-permute-done((bf16[1,512,2560]{2,1,0:T(8,128)(2,1)}, bf16[1,512,2560]{2,1,0:T(8,128)(2,1)S(1)}, u32[]{:S(2)}, u32[]{:S(2)}) %collective-permute-start) | collective-permute-done | bytes 2621472 | tf_op jit(solution)/shard_map/ppermute | solution.py:15
  285.7 4.2 %reduce-scatter.2.cloned.1.call-done = bf16[512,2560]{1,0:T(8,128)(2,1)} async-done(((bf16[512,5120]{1,0:T(8,128)(2,1)}), bf16[512,2560]{1,0:T(8,128)(2,1)}) %reduce-scatter.2.cloned.1.call-update) | async-done | bytes 2621456 | tf_op jit(solution)/shard_map/reduce_scatter | solution.py:105
  289.9 4.0 %fusion.21 = bf16[1,512,2560]{2,1,0:T(8,128)(2,1)} fusion(bf16[512,2560]{1,0:T(8,128)(2,1)} %reduce-scatter.2.cloned.1.call-done, bf16[1,512,2560]{2,1,0:T(8,128)(2,1)S(1)} %collective-permute-done, f32[2560]{0:T(1024)S(1)} %select_reduce_fusion), kind=kLoop, calls=%fused_computation.30 | loop fusion | flops 6553600 | bytes 7874560 | tf_op jit(solution)/shard_map/broadcast_in_dim | solution.py:108
  (16 shorter events, 0.1 us)
Async XLA Ops:
  6.5 34.6 %copy-start.2 = (bf16[1,512,1280]{2,1,0:T(8,128)(2,1)S(1)}, bf16[1,512,1280]{2,1,0:T(8,128)(2,1)}, u32[]{:S(2)}) copy-start(bf16[1,512,1280]{2,1,0:T(8,128)(2,1)} %param.16) | copy-start | bytes 3932164
  6.5 108.3 %all-gather.11.cloned.1.call-start = ((), (), s32[]{:S(2)}) async-start(), calls=%async_computation.4 | async-start | bytes 3932160 | tf_op jit(solution)/shard_map/all_gather | solution.py:68
  8.3 32.8 %collective-permute-start.1 = (bf16[1,512,1280]{1,2,0:T(8,128)(2,1)S(1)}, bf16[1,512,1280]{1,2,0:T(8,128)(2,1)}, u32[]{:S(2)}, u32[]{:S(2)}) collective-permute-start(bf16[1,512,1280]{1,2,0:T(8,128)(2,1)S(1)} %copy.29), channel_id=1, source_target_pairs={{12,0},{0,4},{4,8},{8,12},{13,1},{1,5},{5,9},{9,13},{14,2},{2,6},{... | collective-permute-start | bytes 3932168 | tf_op jit(solution)/shard_map/ppermute | solution.py:15
  41.1 34.5 %copy-start.3 = (bf16[1,512,1280]{2,1,0:T(8,128)(2,1)S(1)}, bf16[1,512,1280]{2,1,0:T(8,128)(2,1)}, u32[]{:S(2)}) copy-start(bf16[1,512,1280]{2,1,0:T(8,128)(2,1)} %param.14) | copy-start | bytes 3932164
  41.1 85.6 %all-gather.13.cloned.1.call-start = ((), (), s32[]{:S(2)}) async-start(), calls=%async_computation.5 | async-start | bytes 3932160 | tf_op jit(solution)/shard_map/all_gather | solution.py:69
  42.6 35.2 %copy-start.6 = (s32[4]{0:T(128)S(1)}, s32[4]{0:T(128)}, u32[]{:S(2)}) copy-start(s32[4]{0:T(128)} %param.22) | copy-start | bytes 52
  42.6 31.1 %collective-permute-start.3 = (bf16[1,512,1280]{1,2,0:T(8,128)(2,1)}, bf16[1,512,1280]{1,2,0:T(8,128)(2,1)S(1)}, u32[]{:S(2)}, u32[]{:S(2)}) collective-permute-start(bf16[1,512,1280]{1,2,0:T(8,128)(2,1)} %copy.33), channel_id=1, source_target_pairs={{12,0},{0,4},{4,8},{8,12},{13,1},{1,5},{5,9},{9,13},{14,2},{2,6},{... | collective-permute-start | bytes 3932168 | tf_op jit(solution)/shard_map/ppermute | solution.py:15
  73.7 1.1 copy-start.4
  74.8 64.4 %all-gather.7.cloned.1.call-start = ((), (), s32[]{:S(2)}) async-start(), calls=%async_computation.1 | async-start | bytes 2949120 | tf_op jit(solution)/shard_map/all_gather | solution.py:78
  75.5 90.3 %all-gather.9.cloned.1.call-start = ((), (), s32[]{:S(2)}) async-start(), calls=%async_computation.2 | async-start | bytes 2949120 | tf_op jit(solution)/shard_map/all_gather | solution.py:79
  77.0 36.3 %collective-permute-start.2 = (bf16[1,512,1280]{1,2,0:T(8,128)(2,1)}, bf16[1,512,1280]{1,2,0:T(8,128)(2,1)S(1)}, u32[]{:S(2)}, u32[]{:S(2)}) collective-permute-start(bf16[1,512,1280]{1,2,0:T(8,128)(2,1)} %copy.30), channel_id=1, source_target_pairs={{12,0},{0,4},{4,8},{8,12},{13,1},{1,5},{5,9},{9,13},{14,2},{2,6},{... | collective-permute-start | bytes 3932168 | tf_op jit(solution)/shard_map/ppermute | solution.py:15
  77.1 212.8 %reduce-scatter.2.cloned.1.call-start = ((), (), s32[]{:S(2)}) async-start(), calls=%async_computation.3 | async-start | bytes 7864320 | tf_op jit(solution)/shard_map/reduce_scatter | solution.py:105
  119.6 7.1 %copy-start.1 = (f32[10,1024,512]{2,1,0:T(8,128)}, f32[10,1024,512]{2,1,0:T(8,128)S(1)}, u32[]{:S(2)}) copy-start(f32[10,1024,512]{2,1,0:T(8,128)S(1)} %get-tuple-element.99) | copy-start | bytes 62914564
  174.2 4.0 %copy-start = (f32[10,512,512]{2,1,0:T(8,128)}, f32[10,512,512]{2,1,0:T(8,128)S(1)}, u32[]{:S(2)}) copy-start(f32[10,512,512]{2,1,0:T(8,128)S(1)} %get-tuple-element.157) | copy-start | bytes 31457284 | tf_op jit(solution)/shard_map/while
  196.2 4.0 %copy-start = (f32[10,512,512]{2,1,0:T(8,128)}, f32[10,512,512]{2,1,0:T(8,128)S(1)}, u32[]{:S(2)}) copy-start(f32[10,512,512]{2,1,0:T(8,128)S(1)} %get-tuple-element.157) | copy-start | bytes 31457284 | tf_op jit(solution)/shard_map/while
  225.4 0.7 copy-start.7
  225.4 1.9 copy-start.5
  225.5 60.2 %collective-permute-start = (bf16[1,512,2560]{2,1,0:T(8,128)(2,1)}, bf16[1,512,2560]{2,1,0:T(8,128)(2,1)S(1)}, u32[]{:S(2)}, u32[]{:S(2)}) collective-permute-start(bf16[1,512,2560]{2,1,0:T(8,128)(2,1)} %param.13), channel_id=1, source_target_pairs={{12,0},{0,4},{4,8},{8,12},{13,1},{1,5},{5,9},{9,13},{14,2},{2,6},{... | collective-permute-start | bytes 7864328 | tf_op jit(solution)/shard_map/ppermute | solution.py:15
Sparse Core Ops, SparseCore 0:
  41.2 11.6 all-gather.10
  74.9 11.1 all-gather.12
  87.7 44.8 all-gather.6
  134.1 31.6 all-gather.8
  225.6 64.2 reduce-scatter.1
where the time goes:
time: 302 us; the launch traced here: 300 us
  waiting for transfers between devices  186 us (62%)
  matrix products  54.1 us (18%)
  local copies, waits for them, and re-layouts  26.8 us (9%)
  other arithmetic  16.7 us (6%)
  between operations  13.9 us (5%)
    ppermute x4, waiting for transfers between devices, shifted(): return lax.ppermute(block, axis, route)  154 us
    dot_general x3, matrix products, attend(): jnp.einsum('thn,nhd->thd', weights, value_heads, preferred_element_type=j...  28.3 us
    all_gather x1, waiting for transfers between devices, on_device(): lax.all_gather(cache_value, ('section', 'seq'), axis=0, tiled=True)  26.6 us
    dot_general x1, matrix products, on_device(): jnp.dot(attended, out_weight, preferred_element_type=jnp.float32)  13.5 us
    dot_general x3, matrix products, attend(): jnp.einsum('thd,nhd->thn', queries, key_heads, preferred_element_type=jnp...  12.3 us
    dynamic_slice x8, local copies, waits for them, and re-layouts, on_device(): lax.scan(block_step, running, (key_rows.reshape(block_count, block_rows,...  10.5 us
    unnamed x17, local copies, waits for them, and re-layouts  9.29 us
    reduce_sum x3, other arithmetic, attend(): total = total * factor + jnp.sum(exponent, axis=2)  7.96 us
  transfers between devices with their start and end apart: 9, of which 6 were waited for; matrix products, arithmetic and copies ran while one was open for 9% of the time, Pallas kernels for 0%

commit v1 on v0

v1 whole, which is shorter than its diff:
```python
import functools
import math

import jax
import jax.numpy as jnp
from jax import lax
from jax.experimental import pallas as pl
from jax.experimental.pallas import tpu as pltpu
from jax.sharding import PartitionSpec as P

HD = 128
MESH = pl.DeviceIdType.MESH
hidden_score = -1e30
to_power = HD ** (-0.5) * math.log2(math.e)
row_chunks = 4
column_parts = 2


def scores_of(queries, keys):
    return lax.dot_general(
        queries, keys, (((1,), (1,)), ((), ())), preferred_element_type=jnp.float32
    )


def weighted(scores, top, values):
    weights = jnp.exp2((scores - top) * to_power).astype(jnp.bfloat16)
    with_ones = jnp.concatenate([values, jnp.ones_like(values)], axis=1)
    return jnp.dot(weights, with_ones, preferred_element_type=jnp.float32)


def kernel(
    sections,
    tensors,
    noise_ref,
    position_ref,
    count_ref,
    query,
    key,
    value,
    cache_key,
    cache_value,
    level_gate,
    weight_hbm,
    hidden_hbm,
    out,
    key_other,
    value_other,
    cache_keys,
    cache_values,
    weight,
    hidden,
    running,
    highest,
    bias,
    gate,
    attended,
    partial_out,
    partial_in,
    partial_own,
    updated,
    local_sem,
    frame_send,
    frame_recv,
    right_send,
    left_send,
    line_recv,
    pair_send,
    pair_recv,
    partial_send,
    partial_recv,
    shift_send,
    shift_recv,
):
    me = lax.axis_index("section")
    core = lax.axis_index("seq")
    group = lax.axis_index("tensor")
    after = lax.rem(me + 1, sections)
    before = lax.rem(me + sections - 1, sections)
    tokens = query.shape[0]
    heads = query.shape[1] // HD
    half_rows = cache_key.shape[0]
    slot_rows = 2 * half_rows
    used = sections - 1
    width = level_gate.shape[1]
    part_width = width // column_parts
    chunk = tokens // row_chunks

    barrier = pltpu.get_barrier_semaphore()
    peers = [{"seq": 1 - core}, {"section": after}, {"section": before}]
    peers += [{"tensor": lax.rem(group + d, tensors)} for d in range(1, tensors)]
    for peer in peers:
        pl.semaphore_signal(barrier, inc=1, device_id=peer, device_id_type=MESH)

    weight_copy = pltpu.make_async_copy(weight_hbm, weight, local_sem.at[0])
    hidden_copy = pltpu.make_async_copy(hidden_hbm.at[0], hidden, local_sem.at[1])
    own_rows = pl.ds(pl.multiple_of(me * slot_rows + core * half_rows, half_rows), half_rows)

    @pl.when(me < used)
    def _():
        cache_keys[own_rows, :] = cache_key[...]
        cache_values[own_rows, :] = cache_value[...]

    pl.semaphore_wait(barrier, len(peers))

    def line_copies(slot, sends, target):
        rows = pl.ds(pl.multiple_of(slot * slot_rows + core * half_rows, half_rows), half_rows)
        return [
            pltpu.make_async_remote_copy(
                src_ref=rows_of.at[rows],
                dst_ref=rows_of.at[rows],
                send_sem=sends.at[which, slot],
                recv_sem=(pair_recv if sends is pair_send else line_recv).at[which, slot],
                device_id=target,
                device_id_type=MESH,
            )
            for which, rows_of in enumerate((cache_keys, cache_values))
        ]

    def to_right(slot):
        return line_copies(slot, right_send, {"section": after})

    def to_left(slot):
        return line_copies(slot, left_send, {"section": before})

    def to_pair(slot):
        return line_copies(slot, pair_send, {"seq": 1 - core})

    def start(copies):
        for copy in copies:
            copy.start()

    def pair_arrived(slot):
        rows = pl.ds(
            pl.multiple_of(slot * slot_rows + (1 - core) * half_rows, half_rows), half_rows
        )
        for which, rows_of in enumerate((cache_keys, cache_values)):
            pltpu.make_async_remote_copy(
                src_ref=rows_of.at[rows],
                dst_ref=rows_of.at[rows],
                send_sem=pair_send.at[which, slot],
                recv_sem=pair_recv.at[which, slot],
                device_id={"seq": 1 - core},
                device_id_type=MESH,
            ).wait_recv()

    frame_copies = [
        pltpu.make_async_remote_copy(
            src_ref=source,
            dst_ref=landing,
            send_sem=frame_send.at[which],
            recv_sem=frame_recv.at[which],
            device_id={"seq": 1 - core},
            device_id_type=MESH,
        )
        for which, (source, landing) in enumerate(((key, key_other), (value, value_other)))
    ]

    @pl.when(me < used)
    def _():
        start(to_right(me))

    @pl.when((me >= 1) & (me < used))
    def _():
        start(to_left(me))

    start(frame_copies)

    @pl.when(me < used)
    def _():
        start(to_pair(me))

    weight_copy.start()
    hidden_copy.start()

    def relay(step, carry):
        from_left = me - 1 - step
        from_right = me + 1 + step

        @pl.when(from_left >= 0)
        def _():
            for copy in to_right(from_left):
                copy.wait_recv()

            @pl.when(me < used)
            def _():
                start(to_right(from_left))

            start(to_pair(from_left))

        @pl.when(from_right < used)
        def _():
            for copy in to_left(from_right):
                copy.wait_recv()

            @pl.when(me >= 1)
            def _():
                start(to_left(from_right))

            start(to_pair(from_right))

        return carry

    limit = jnp.minimum(count_ref[0], position_ref[me] * slot_rows)
    row = lax.broadcasted_iota(jnp.int32, bias.shape, 1)
    bias[...] = jnp.where(row < limit, 0.0, hidden_score)
    level = lax.broadcasted_iota(jnp.int32, level_gate.shape, 0)
    gate[...] = jnp.sum(
        jnp.where(level == noise_ref[me], level_gate[...], 0.0), axis=0, keepdims=True
    )

    for copy in frame_copies:
        copy.wait_recv()
    block = min(tokens, 256)

    def frame_head(h, carry):
        columns = pl.ds(pl.multiple_of(h * HD, HD), HD)
        for first in range(0, tokens, block):
            rows = pl.ds(first, block)
            queries = query[rows, columns]
            near = scores_of(queries, key[:, columns])
            far = scores_of(queries, key_other[:, columns])
            top = jnp.max(jnp.maximum(near, far), axis=1, keepdims=True)
            running[h, rows, :] = weighted(near, top, value[:, columns]) + weighted(
                far, top, value_other[:, columns]
            )
            highest[h, rows, :] = jnp.broadcast_to(top, (block, HD))
        return carry

    early = max(1, (heads * 7) // 10)
    lax.fori_loop(0, early, frame_head, 0)
    relay(0, 0)
    lax.fori_loop(early, heads, frame_head, 0)
    lax.fori_loop(1, used, relay, 0)

    def slot_ready(slot, carry):
        pair_arrived(slot)
        return carry

    lax.fori_loop(0, used, slot_ready, 0)
    weight_copy.wait()
    hidden_copy.wait()

    def partial_copy(d, unit):
        return pltpu.make_async_remote_copy(
            src_ref=partial_out.at[d - 1, unit],
            dst_ref=partial_in.at[d - 1, unit],
            send_sem=partial_send.at[d - 1, unit],
            recv_sem=partial_recv.at[d - 1, unit],
            device_id={"tensor": lax.rem(group + d, tensors)},
            device_id_type=MESH,
        )

    def shift_copy(c, part):
        unit = c * column_parts + part
        rows = pl.ds(pl.multiple_of(c * chunk, chunk), chunk)
        return pltpu.make_async_remote_copy(
            src_ref=updated.at[unit],
            dst_ref=out.at[0, rows, pl.ds(part * part_width, part_width)],
            send_sem=shift_send.at[unit],
            recv_sem=shift_recv.at[unit],
            device_id={"section": after},
            device_id_type=MESH,
        )

    def combine(c):
        rows = pl.ds(pl.multiple_of(c * chunk, chunk), chunk)
        for part in range(column_parts):
            unit = c * column_parts + part
            columns = pl.ds(part * part_width, part_width)
            branch = partial_own[unit].astype(jnp.float32)
            for d in range(1, tensors):
                partial_copy(d, unit).wait_recv()
                branch = branch + partial_in[d - 1, unit].astype(jnp.float32)
            updated[unit] = (
                hidden[rows, columns].astype(jnp.float32) + gate[:, columns] * branch
            ).astype(jnp.bfloat16)
            shift_copy(c, part).start()

    def row_step(c, carry):
        rows = pl.ds(pl.multiple_of(c * chunk, chunk), chunk)

        def cache_head(h, inner):
            columns = pl.ds(pl.multiple_of(h * HD, HD), HD)
            scores = scores_of(query[rows, columns], cache_keys[:, columns]) + bias[...]
            old_top = highest[h, rows, :]
            top = jnp.maximum(old_top, jnp.max(scores, axis=1, keepdims=True))
            factor = jnp.exp2((old_top - top) * to_power)
            total = weighted(scores, top[:, :1], cache_values[:, columns])
            old = running[h, rows, :]
            summed = old[:, :HD] * factor + total[:, :HD]
            weight_sum = old[:, HD:] * factor + total[:, HD:]
            attended[:, columns] = (summed / weight_sum).astype(jnp.bfloat16)
            return inner

        lax.fori_loop(0, heads, cache_head, 0)

        def project(owner, part):
            columns = pl.ds(pl.multiple_of(owner * width + part * part_width, HD), part_width)
            return jnp.dot(
                attended[...], weight[:, columns], preferred_element_type=jnp.float32
            ).astype(jnp.bfloat16)

        for part in range(column_parts):
            unit = c * column_parts + part
            for d in range(1, tensors):
                partial_out[d - 1, unit] = project(lax.rem(group + d, tensors), part)
                partial_copy(d, unit).start()
        for part in range(column_parts):
            partial_own[c * column_parts + part] = project(group, part)

        @pl.when(c >= 1)
        def _():
            combine(c - 1)

        return carry

    lax.fori_loop(0, row_chunks, row_step, 0)
    combine(row_chunks - 1)

    for copy in frame_copies:
        copy.wait_send()

    def slot_sent(slot, carry):
        @pl.when((slot <= me) & (me < used))
        def _():
            for copy in to_right(slot):
                copy.wait_send()

        @pl.when((slot >= me) & (me >= 1))
        def _():
            for copy in to_left(slot):
                copy.wait_send()

        for copy in to_pair(slot):
            copy.wait_send()
        return carry

    lax.fori_loop(0, used, slot_sent, 0)

    def chunk_done(c, carry):
        for part in range(column_parts):
            for d in range(1, tensors):
                partial_copy(d, c * column_parts + part).wait_send()
            shift_copy(c, part).wait()
        return carry

    lax.fori_loop(0, row_chunks, chunk_done, 0)


def on_device(
    hidden_state,
    frame_query,
    frame_key,
    frame_value,
    cache_key,
    cache_value,
    out_weight,
    level_gate,
    noise_level,
    frame_position,
    cached_count,
):
    sections = lax.axis_size("section")
    tensors = lax.axis_size("tensor")
    tokens, inner = frame_query.shape[1:]
    heads = inner // HD
    width = hidden_state.shape[2]
    used_rows = (sections - 1) * 2 * cache_key.shape[0]
    units = row_chunks * column_parts
    chunk = tokens // row_chunks
    piece = (chunk, width // column_parts)
    bf16, f32 = jnp.bfloat16, jnp.float32
    scalars = pl.BlockSpec(memory_space=pltpu.SMEM)
    near = pl.BlockSpec(memory_space=pltpu.VMEM)
    far = pl.BlockSpec(memory_space=pl.ANY)
    dma = pltpu.SemaphoreType.DMA
    return pl.pallas_call(
        functools.partial(kernel, sections, tensors),
        out_shape=jax.ShapeDtypeStruct(hidden_state.shape, bf16),
        in_specs=[scalars] * 3 + [near] * 6 + [far] * 2,
        out_specs=far,
        scratch_shapes=[
            pltpu.VMEM((tokens, inner), bf16),
            pltpu.VMEM((tokens, inner), bf16),
            pltpu.VMEM((used_rows, inner), bf16),
            pltpu.VMEM((used_rows, inner), bf16),
            pltpu.VMEM(out_weight.shape, bf16),
            pltpu.VMEM((tokens, width), bf16),
            pltpu.VMEM((heads, tokens, 2 * HD), f32),
            pltpu.VMEM((heads, tokens, HD), f32),
            pltpu.VMEM((1, used_rows), f32),
            pltpu.VMEM((1, width), f32),
            pltpu.VMEM((chunk, inner), bf16),
            pltpu.VMEM((tensors - 1, units) + piece, bf16),
            pltpu.VMEM((tensors - 1, units) + piece, bf16),
            pltpu.VMEM((units,) + piece, bf16),
            pltpu.VMEM((units,) + piece, bf16),
            dma((2,)),
            dma((2,)),
            dma((2,)),
            dma((2, sections - 1)),
            dma((2, sections - 1)),
            dma((2, sections - 1)),
            dma((2, sections - 1)),
            dma((2, sections - 1)),
            dma((tensors - 1, units)),
            dma((tensors - 1, units)),
            dma((units,)),
            dma((units,)),
        ],
        compiler_params=pltpu.CompilerParams(
            collective_id=0, has_side_effects=True, vmem_limit_bytes=60 * 1024 * 1024
        ),
    )(
        noise_level,
        frame_position,
        cached_count,
        frame_query[0],
        frame_key[0],
        frame_value[0],
        cache_key,
        cache_value,
        level_gate,
        out_weight,
        hidden_state,
    )


def solution(mesh):
    placed = (
        P(("parts", "section"), "seq", "tensor"),
        P(("parts", "section"), "seq", "tensor"),
        P(("parts", "section"), "seq", "tensor"),
        P(("parts", "section"), "seq", "tensor"),
        P(("parts", "section", "seq"), "tensor"),
        P(("parts", "section", "seq"), "tensor"),
        P("tensor", None),
        P(None, "tensor"),
        P("parts"),
        P("parts"),
        P("parts"),
    )
    return jax.shard_map(
        on_device,
        mesh=mesh,
        in_specs=placed,
        out_specs=P(("parts", "section"), "seq", "tensor"),
        check_vma=False,
    )
```

time: 302 us -> 134 us (0.44)
  waiting for transfers between devices: 186 us -> 0 us
  Pallas kernels: 0 us -> 130 us
  matrix products: 54.1 us -> 0 us
  local copies, waits for them, and re-layouts: 26.8 us -> 3.4 us
  other arithmetic: 16.7 us -> 0 us
  between operations: 13.9 us -> 0.66 us
    ppermute x4 -> x0, waiting for transfers between devices: 154 us -> none  [shifted(): return lax.ppermute(block, axis, route)]
    pallas_call x0 -> x1, Pallas kernels: none -> 130 us  [on_device(): pl.pallas_call(functools.partial(kernel, sections, tensors), out_shape=ja...]
    dot_general x7 -> x0, matrix products: 54.1 us -> none  [the longest x3 28.3 us: attend(): jnp.einsum('thn,nhd->thd', weights, value_heads, preferred_element_type=j...]
    all_gather x4 -> x0, waiting for transfers between devices: 26.7 us -> none  [the longest x1 26.6 us: on_device(): lax.all_gather(cache_value, ('section', 'seq'), axis=0, tiled=True)]
    dynamic_slice x8 -> x0, local copies, waits for them, and re-layouts: 10.5 us -> none  [on_device(): lax.scan(block_step, running, (key_rows.reshape(block_count, block_rows,...]
    reduce_sum x6 -> x0, other arithmetic: 9.29 us -> none  [the longest x3 7.96 us: attend(): total = total * factor + jnp.sum(exponent, axis=2)]
    while x8 -> x0, local copies, waits for them, and re-layouts: 7.06 us -> none  [the longest x2 3.59 us: on_device(): lax.scan(block_step, running, (key_rows.reshape(block_count, block_rows,...]
    unnamed x17 -> x1, local copies, waits for them, and re-layouts: 9.29 us -> 3.4 us
  transfers between devices with their start and end apart: 9 -> 0, of which waited for: 6 -> 0; matrix products, arithmetic and copies ran while one was open for 9% -> 0% of each run, Pallas kernels for 0% -> 0%
where the time goes in v1:
time: 134 us
  Pallas kernels  130 us (97%)
  local copies, waits for them, and re-layouts  3.4 us (3%)
    pallas_call x1, Pallas kernels, on_device(): pl.pallas_call(functools.partial(kernel, sections, tensors), out_shape=ja...  130 us
    unnamed x1, local copies, waits for them, and re-layouts  3.4 us

profile of v1, /device:TPU:1, one launch (start us, length us, event | category | flops | bytes accessed | tf_op | source)
XLA Modules:
  0.0 133.6 jit_solution(8878351069217793151)
XLA Ops:
  0.7 129.6 %shard_map.109 = bf16[1,512,2560]{2,1,0:T(8,128)(2,1)} custom-call(s32[4]{0:T(128)} %noise_ref.1, s32[4]{0:T(128)} %position_ref.1, s32[1]{0:T(128)S(6)} %copy.13.count_ref, bf16[512,1280]{1,0:T(8,128)(2,1)} %bitcast.3, bf16[512,1280]{1,0:T(8,128)(2,1)} %bitcast.4, bf16[512,1280]{1,0:T(8,128)(2,1)} %bitcast.5, bf16[128,1280]{1,0:T(8,128)(2,1)} %cache_key.1, ...), custom_call_target="tpu_custom_call" | custom-call | tf_op jit(solution)/shard_map/pallas_call | solution.py:377
  130.2 3.4 %copy.14 = bf16[1,512,2560]{2,1,0:T(8,128)(2,1)} copy(bf16[1,512,2560]{2,1,0:T(8,128)(2,1)} %shard_map.109) | data formatting | bytes 5242880

commit v2 on v1

--- a/solution.py
+++ b/solution.py
@@ -13,7 +13,8 @@
 hidden_score = -1e30
 to_power = HD ** (-0.5) * math.log2(math.e)
 row_chunks = 4
-column_parts = 2
+column_parts = 5
+lag = 2
 
 
 def scores_of(queries, keys):
@@ -51,7 +52,6 @@
     hidden,
     running,
     highest,
-    bias,
     gate,
     attended,
     partial_out,
@@ -102,28 +102,26 @@
 
     pl.semaphore_wait(barrier, len(peers))
 
-    def line_copies(slot, sends, target):
+    def line_copy(slot, which, sends, target):
         rows = pl.ds(pl.multiple_of(slot * slot_rows + core * half_rows, half_rows), half_rows)
-        return [
-            pltpu.make_async_remote_copy(
-                src_ref=rows_of.at[rows],
-                dst_ref=rows_of.at[rows],
-                send_sem=sends.at[which, slot],
-                recv_sem=(pair_recv if sends is pair_send else line_recv).at[which, slot],
-                device_id=target,
-                device_id_type=MESH,
-            )
-            for which, rows_of in enumerate((cache_keys, cache_values))
-        ]
-
-    def to_right(slot):
-        return line_copies(slot, right_send, {"section": after})
-
-    def to_left(slot):
-        return line_copies(slot, left_send, {"section": before})
-
-    def to_pair(slot):
-        return line_copies(slot, pair_send, {"seq": 1 - core})
+        rows_of = (cache_keys, cache_values)[which]
+        return pltpu.make_async_remote_copy(
+            src_ref=rows_of.at[rows],
+            dst_ref=rows_of.at[rows],
+            send_sem=sends.at[which, slot],
+            recv_sem=(pair_recv if sends is pair_send else line_recv).at[which, slot],
+            device_id=target,
+            device_id_type=MESH,
+        )
+
+    def to_right(slot, kinds=(0, 1)):
+        return [line_copy(slot, which, right_send, {"section": after}) for which in kinds]
+
+    def to_left(slot, kinds=(0, 1)):
+        return [line_copy(slot, which, left_send, {"section": before}) for which in kinds]
+
+    def to_pair(slot, kinds=(0, 1)):
+        return [line_copy(slot, which, pair_send, {"seq": 1 - core}) for which in kinds]
 
     def start(copies):
         for copy in copies:
@@ -172,71 +170,115 @@
     weight_copy.start()
     hidden_copy.start()
 
-    def relay(step, carry):
+    def relay(step, which):
         from_left = me - 1 - step
         from_right = me + 1 + step
 
         @pl.when(from_left >= 0)
         def _():
-            for copy in to_right(from_left):
-                copy.wait_recv()
+            to_right(from_left, (which,))[0].wait_recv()
 
             @pl.when(me < used)
             def _():
-                start(to_right(from_left))
-
-            start(to_pair(from_left))
+                start(to_right(from_left, (which,)))
+
+            start(to_pair(from_left, (which,)))
 
         @pl.when(from_right < used)
         def _():
-            for copy in to_left(from_right):
-                copy.wait_recv()
+            to_left(from_right, (which,))[0].wait_recv()
 
             @pl.when(me >= 1)
             def _():
-                start(to_left(from_right))
-
-            start(to_pair(from_right))
-
-        return carry
+                start(to_left(from_right, (which,)))
+
+            start(to_pair(from_right, (which,)))
 
     limit = jnp.minimum(count_ref[0], position_ref[me] * slot_rows)
-    row = lax.broadcasted_iota(jnp.int32, bias.shape, 1)
-    bias[...] = jnp.where(row < limit, 0.0, hidden_score)
+    row = lax.broadcasted_iota(jnp.int32, (1, slot_rows), 1)
     level = lax.broadcasted_iota(jnp.int32, level_gate.shape, 0)
     gate[...] = jnp.sum(
         jnp.where(level == noise_ref[me], level_gate[...], 0.0), axis=0, keepdims=True
     )
 
-    for copy in frame_copies:
-        copy.wait_recv()
     block = min(tokens, 256)
 
-    def frame_head(h, carry):
+    def near_head(h, carry):
         columns = pl.ds(pl.multiple_of(h * HD, HD), HD)
         for first in range(0, tokens, block):
             rows = pl.ds(first, block)
-            queries = query[rows, columns]
-            near = scores_of(queries, key[:, columns])
-            far = scores_of(queries, key_other[:, columns])
-            top = jnp.max(jnp.maximum(near, far), axis=1, keepdims=True)
-            running[h, rows, :] = weighted(near, top, value[:, columns]) + weighted(
-                far, top, value_other[:, columns]
-            )
+            scores = scores_of(query[rows, columns], key[:, columns])
+            top = jnp.max(scores, axis=1, keepdims=True)
+            running[h, rows, :] = weighted(scores, top, value[:, columns])
             highest[h, rows, :] = jnp.broadcast_to(top, (block, HD))
         return carry
 
-    early = max(1, (heads * 7) // 10)
-    lax.fori_loop(0, early, frame_head, 0)
+    def merged(scores, values, h, rows):
+        old_top = highest[h, rows, :]
+        top = jnp.maximum(old_top, jnp.max(scores, axis=1, keepdims=True))
+        factor = jnp.exp2((old_top - top) * to_power)
+        total = weighted(scores, top[:, :1], values)
+        old = running[h, rows, :]
+        return (
+            old[:, :HD] * factor + total[:, :HD],
+            old[:, HD:] * factor + total[:, HD:],
+            top,
+        )
+
+    def keep(state, h, rows):
+        running[h, rows, :] = jnp.concatenate(state[:2], axis=1)
+        highest[h, rows, :] = state[2]
+
+    def far_head(h, carry):
+        columns = pl.ds(pl.multiple_of(h * HD, HD), HD)
+        for first in range(0, tokens, block):
+            rows = pl.ds(first, block)
+            scores = scores_of(query[rows, columns], key_other[:, columns])
+            keep(merged(scores, value_other[:, columns], h, rows), h, rows)
+        return carry
+
+    def with_slot(slot, h, rows):
+        columns = pl.ds(pl.multiple_of(h * HD, HD), HD)
+        slot_at = pl.ds(pl.multiple_of(slot * slot_rows, slot_rows), slot_rows)
+        bias = jnp.where(row < limit - slot * slot_rows, 0.0, hidden_score)
+        scores = scores_of(query[rows, columns], cache_keys[slot_at, columns]) + bias
+        return merged(scores, cache_values[slot_at, columns], h, rows)
+
+    final = jnp.where(2 * me >= used - 1, 0, used - 1)
+
+    def take_slot(slot):
+        @pl.when((slot >= 0) & (slot < used) & (slot != final))
+        def _():
+            pair_arrived(slot)
+
+            def slot_head(h, carry):
+                for first in range(0, tokens, block):
+                    rows = pl.ds(first, block)
+                    keep(with_slot(slot, h, rows), h, rows)
+                return carry
+
+            lax.fori_loop(0, heads, slot_head, 0)
+
+    def slot_step(step, carry):
+        relay(step, 0)
+        take_slot(me - step)
+        relay(step, 1)
+        take_slot(me + step)
+        return carry
+
+    early = max(1, (heads * 2) // 5)
+    lax.fori_loop(0, heads, near_head, 0)
     relay(0, 0)
-    lax.fori_loop(early, heads, frame_head, 0)
-    lax.fori_loop(1, used, relay, 0)
-
-    def slot_ready(slot, carry):
-        pair_arrived(slot)
-        return carry
-
-    lax.fori_loop(0, used, slot_ready, 0)
+    for copy in frame_copies:
+        copy.wait_recv()
+    lax.fori_loop(0, early, far_head, 0)
+    relay(0, 1)
+    lax.fori_loop(early, heads, far_head, 0)
+    take_slot(me)
+    lax.fori_loop(1, used, slot_step, 0)
+    take_slot(me - used)
+    take_slot(me + used)
+    pair_arrived(final)
     weight_copy.wait()
     hidden_copy.wait()
 
@@ -262,37 +304,37 @@
             device_id_type=MESH,
         )
 
-    def combine(c):
+    def combine(c, part):
         rows = pl.ds(pl.multiple_of(c * chunk, chunk), chunk)
-        for part in range(column_parts):
-            unit = c * column_parts + part
-            columns = pl.ds(part * part_width, part_width)
-            branch = partial_own[unit].astype(jnp.float32)
-            for d in range(1, tensors):
-                partial_copy(d, unit).wait_recv()
-                branch = branch + partial_in[d - 1, unit].astype(jnp.float32)
-            updated[unit] = (
-                hidden[rows, columns].astype(jnp.float32) + gate[:, columns] * branch
-            ).astype(jnp.bfloat16)
-            shift_copy(c, part).start()
+        unit = c * column_parts + part
+        columns = pl.ds(part * part_width, part_width)
+        branch = partial_own[unit].astype(jnp.float32)
+        for d in range(1, tensors):
+            partial_copy(d, unit).wait_recv()
+            branch = branch + partial_in[d - 1, unit].astype(jnp.float32)
+        updated[unit] = (
+            hidden[rows, columns].astype(jnp.float32) + gate[:, columns] * branch
+        ).astype(jnp.bfloat16)
+        shift_copy(c, part).start()
+
+    def right_sent(slot, carry):
+        @pl.when((slot <= me) & (me < used))
+        def _():
+            for copy in to_right(slot):
+                copy.wait_send()
+
+        return carry
 
     def row_step(c, carry):
         rows = pl.ds(pl.multiple_of(c * chunk, chunk), chunk)
 
-        def cache_head(h, inner):
+        def last_slot_head(h, inner):
             columns = pl.ds(pl.multiple_of(h * HD, HD), HD)
-            scores = scores_of(query[rows, columns], cache_keys[:, columns]) + bias[...]
-            old_top = highest[h, rows, :]
-            top = jnp.maximum(old_top, jnp.max(scores, axis=1, keepdims=True))
-            factor = jnp.exp2((old_top - top) * to_power)
-            total = weighted(scores, top[:, :1], cache_values[:, columns])
-            old = running[h, rows, :]
-            summed = old[:, :HD] * factor + total[:, :HD]
-            weight_sum = old[:, HD:] * factor + total[:, HD:]
+            summed, weight_sum, top = with_slot(final, h, rows)
             attended[:, columns] = (summed / weight_sum).astype(jnp.bfloat16)
             return inner
 
-        lax.fori_loop(0, heads, cache_head, 0)
+        lax.fori_loop(0, heads, last_slot_head, 0)
 
         def project(owner, part):
             columns = pl.ds(pl.multiple_of(owner * width + part * part_width, HD), part_width)
@@ -305,27 +347,30 @@
             for d in range(1, tensors):
                 partial_out[d - 1, unit] = project(lax.rem(group + d, tensors), part)
                 partial_copy(d, unit).start()
-        for part in range(column_parts):
-            partial_own[c * column_parts + part] = project(group, part)
-
-        @pl.when(c >= 1)
-        def _():
-            combine(c - 1)
+            partial_own[unit] = project(group, part)
+            if part == lag:
+                @pl.when(c == 0)
+                def _():
+                    lax.fori_loop(0, used, right_sent, 0)
+
+            if part >= lag:
+                combine(c, part - lag)
+            else:
+
+                @pl.when(c >= 1)
+                def _():
+                    combine(c - 1, column_parts + part - lag)
 
         return carry
 
     lax.fori_loop(0, row_chunks, row_step, 0)
-    combine(row_chunks - 1)
+    for part in range(column_parts - lag, column_parts):
+        combine(row_chunks - 1, part)
 
     for copy in frame_copies:
         copy.wait_send()
 
     def slot_sent(slot, carry):
-        @pl.when((slot <= me) & (me < used))
-        def _():
-            for copy in to_right(slot):
-                copy.wait_send()
-
         @pl.when((slot >= me) & (me >= 1))
         def _():
             for copy in to_left(slot):
@@ -388,7 +433,6 @@
             pltpu.VMEM((tokens, width), bf16),
             pltpu.VMEM((heads, tokens, 2 * HD), f32),
             pltpu.VMEM((heads, tokens, HD), f32),
-            pltpu.VMEM((1, used_rows), f32),
             pltpu.VMEM((1, width), f32),
             pltpu.VMEM((chunk, inner), bf16),
             pltpu.VMEM((tensors - 1, units) + piece, bf16),

time: 134 us -> 129 us (0.963)
  Pallas kernels: 130 us -> 125 us
    pallas_call x1, Pallas kernels: 130 us -> 125 us  [on_device(): pl.pallas_call(functools.partial(kernel, sections, tensors), out_shape=ja...]
where the time goes in v2:
time: 129 us
  Pallas kernels  125 us (97%)
  local copies, waits for them, and re-layouts  3.4 us (3%)
    pallas_call x1, Pallas kernels, on_device(): pl.pallas_call(functools.partial(kernel, sections, tensors), out_shape=ja...  125 us
    unnamed x1, local copies, waits for them, and re-layouts  3.4 us

profile of v2, /device:TPU:1, one launch (start us, length us, event | category | flops | bytes accessed | tf_op | source)
XLA Modules:
  0.0 129.3 jit_solution(6869416426337155319)
XLA Ops:
  0.7 125.2 %shard_map.109 = bf16[1,512,2560]{2,1,0:T(8,128)(2,1)} custom-call(s32[4]{0:T(128)} %noise_ref.1, s32[4]{0:T(128)} %position_ref.1, s32[1]{0:T(128)S(6)} %copy.13.count_ref, bf16[512,1280]{1,0:T(8,128)(2,1)} %bitcast.3, bf16[512,1280]{1,0:T(8,128)(2,1)} %bitcast.4, bf16[512,1280]{1,0:T(8,128)(2,1)} %bitcast.5, bf16[128,1280]{1,0:T(8,128)(2,1)} %cache_key.1, ...), custom_call_target="tpu_custom_call" | custom-call | tf_op jit(solution)/shard_map/pallas_call | solution.py:422
  125.9 3.4 %copy.14 = bf16[1,512,2560]{2,1,0:T(8,128)(2,1)} copy(bf16[1,512,2560]{2,1,0:T(8,128)(2,1)} %shard_map.109) | data formatting | bytes 5242880
